TPU v7x, 256 devices: a whole 4x4x8 slice. The times are simulated.
256 devices in a mesh: rows: 32 (over z, x), cols: 8 (over y, core).
Axes of the slice: x: 4, y: 4, z: 8, core: 2. Of those that a mesh axis runs over, the one named last changes fastest.
Arguments:
- panel: float32 [131072, 256], P('rows'), may hold values from -0.099436891 to 0.099436891
- trailing: float32 [131072, 1024], P('rows', 'cols'), may hold values from -6 to 6
Outputs:
- factor_r: float32 [256, 256], replicated
- projected: float32 [256, 1024], P(None, 'cols')
- remainder: float32 [131072, 1024], P('rows', 'cols')
All inputs are finite; a program needn't handle non-finite values.
Results may differ from a plain program's by a relative error of at most 0.0003.
Values sent between devices are 32-bit elements; how exact they have to be, the bound alone decides.
No kernel may reach another device: no remote copies, remote signals or barrier semaphores. Data moves between devices by JAX's collectives and lax.ppermute only.
A program may use at most 64 MiB of HBM per device.

v0:
```python
import jax
import jax.numpy as jnp
from jax import lax
from jax.sharding import PartitionSpec as P


def product(left, right):
    return jnp.dot(left, right, precision=lax.Precision.HIGHEST, preferred_element_type=jnp.float32)


def inner(left, right):
    return lax.dot_general(
        left,
        right,
        (((0,), (0,)), ((), ())),
        precision=lax.Precision.HIGHEST,
        preferred_element_type=jnp.float32,
    )


def gram_of(left):
    return lax.psum(inner(left, left), "rows")


def lower_inverse(gram):
    lower = jnp.linalg.cholesky(gram)
    identity = jnp.eye(gram.shape[0], dtype=jnp.float32)
    inverse = lax.linalg.triangular_solve(lower, identity, left_side=True, lower=True)
    return (lower, inverse)


def on_device(panel, trailing):
    lower_one, inverse_one = lower_inverse(gram_of(panel))
    first_basis = product(panel, inverse_one.T)
    lower_two, inverse_two = lower_inverse(gram_of(first_basis))
    basis = product(first_basis, inverse_two.T)
    projected = lax.psum(inner(basis, trailing), "rows")
    factor_r = product(lower_two.T, lower_one.T)
    remainder = trailing - product(basis, projected)
    return (factor_r, projected, remainder)


def solution(mesh):
    return jax.shard_map(
        on_device,
        mesh=mesh,
        in_specs=(P("rows", None), P("rows", "cols")),
        out_specs=(P(), P(None, "cols"), P("rows", "cols")),
        check_vma=False,
    )
```

profile of v0, /device:TPU:1, one launch (start us, length us, event | category | flops | bytes accessed | tf_op | source)
XLA Modules:
  0.0 612.7 jit_solution(15561777920822254100)
XLA Ops:
  7.2 0.0 all-reduce.5.cloned.1.call-start
  7.2 10.9 %fusion.44 = f32[256,256]{0,1:T(8,128)} fusion(f32[4096,256]{1,0:T(8,128)} %param.5), kind=kOutput, calls=%fused_computation.76 | convolution fusion | flops 3221225472 | bytes 4456448 | tf_op jit(solution)/shard_map/dot_general | solution.py:12
  18.1 0.0 all-reduce.5.cloned.1.call-update
  18.1 0.2 all-reduce.7.cloned.1.call-start
  18.4 143.3 %all-reduce.5.cloned.1.call-done = f32[256,256]{0,1:T(8,128)} async-done(((f32[256,256]{0,1:T(8,128)}), f32[256,256]{0,1:T(8,128)}) %all-reduce.5.cloned.1.call-update) | async-done | bytes 262160 | tf_op jit(solution)/shard_map/psum | solution.py:22
  161.7 1.1 copy.6
  162.8 1.0 fusion.9
  163.8 11.7 %cholesky.130 = f32[128,128]{1,0:T(8,128)S(1)} custom-call(f32[128,128]{1,0:T(8,128)S(1)} %cholesky.194), custom_call_target="Cholesky" | custom-call | tf_op jit(solution)/shard_map/jit(cholesky)/cholesky | solution.py:26
  175.5 9.8 %custom-call.13 = f32[1,128,128]{1,2,0:T(8,128)S(1)} custom-call(f32[1,128,128]{2,1,0:T(8,128)S(1)} %get-tuple-element.48), custom_call_target="InvertDiagBlocksLowerTriangular" | custom-call | tf_op jit(solution)/shard_map/jit(cholesky)/cholesky | solution.py:26
  185.4 0.2 constant_dynamic-update-slice_fusion.3
  185.6 0.3 convolution_subtract_fusion.4
  185.8 11.7 %cholesky.147 = f32[128,128]{1,0:T(8,128)S(1)} custom-call(f32[128,128]{1,0:T(8,128)S(1)} %convolution_subtract_fusion.4), custom_call_target="Cholesky" | custom-call | tf_op jit(solution)/shard_map/jit(cholesky)/cholesky | solution.py:26
  197.6 0.7 compare_reduce_fusion.2
  199.7 0.1 broadcast.89
  199.8 4.3 while.4
  200.0 0.6 fusion.67
  200.6 1.4 bitcast_dynamic-update-slice_fusion.4
  202.1 0.6 fusion.67
  202.7 1.4 bitcast_dynamic-update-slice_fusion.4
  204.1 19.7 %custom-call.14 = f32[2,128,128]{1,2,0:T(8,128)S(1)} custom-call(f32[2,128,128]{2,1,0:T(8,128)S(1)} %get-tuple-element.19), custom_call_target="InvertDiagBlocksLowerTriangular" | custom-call | tf_op jit(solution)/shard_map/triangular_solve/custom-call.0 | solution.py:28
  223.8 0.3 fusion.22
  224.1 0.3 convolution_subtract_fusion.2
  224.4 0.3 fusion.29
  224.7 5.5 fusion
  230.2 0.0 copy-start
  230.2 1.9 copy-done
  232.1 4.2 fusion.45
  236.4 0.0 all-reduce.7.cloned.1.call-update
  236.4 0.3 all-reduce.9.cloned.1.call-start
  236.7 140.9 %all-reduce.7.cloned.1.call-done = f32[256,256]{0,1:T(8,128)} async-done(((f32[256,256]{0,1:T(8,128)}), f32[256,256]{0,1:T(8,128)}) %all-reduce.7.cloned.1.call-update) | async-done | bytes 262160 | tf_op jit(solution)/shard_map/psum | solution.py:22
  377.5 1.1 copy.8
  378.6 1.0 fusion.8
  379.6 11.7 %cholesky.164 = f32[128,128]{1,0:T(8,128)S(1)} custom-call(f32[128,128]{1,0:T(8,128)S(1)} %cholesky.197), custom_call_target="Cholesky" | custom-call | tf_op jit(solution)/shard_map/jit(cholesky)/cholesky | solution.py:26
  391.4 0.6 compare_reduce_fusion.1
  392.0 9.8 %custom-call.15 = f32[1,128,128]{1,2,0:T(8,128)S(1)} custom-call(f32[1,128,128]{2,1,0:T(8,128)S(1)} %get-tuple-element.44), custom_call_target="InvertDiagBlocksLowerTriangular" | custom-call | tf_op jit(solution)/shard_map/jit(cholesky)/cholesky | solution.py:26
  401.9 0.2 constant_dynamic-update-slice_fusion.1
  402.1 0.3 convolution_subtract_fusion.3
  402.3 11.7 %cholesky.181 = f32[128,128]{1,0:T(8,128)S(1)} custom-call(f32[128,128]{1,0:T(8,128)S(1)} %convolution_subtract_fusion.3), custom_call_target="Cholesky" | custom-call | tf_op jit(solution)/shard_map/jit(cholesky)/cholesky | solution.py:26
  414.1 0.6 compare_reduce_fusion
  416.1 4.5 while.5
  416.6 0.6 fusion.68
  417.2 1.4 bitcast_dynamic-update-slice_fusion.5
  418.6 0.6 fusion.68
  419.2 1.4 bitcast_dynamic-update-slice_fusion.5
  420.6 19.7 %custom-call.16 = f32[2,128,128]{1,2,0:T(8,128)S(1)} custom-call(f32[2,128,128]{2,1,0:T(8,128)S(1)} %get-tuple-element.20), custom_call_target="InvertDiagBlocksLowerTriangular" | custom-call | tf_op jit(solution)/shard_map/triangular_solve/custom-call.0 | solution.py:28
  440.2 0.3 fusion.20
  440.6 0.3 convolution_subtract_fusion.1
  440.8 0.3 fusion.25
  441.1 0.0 copy-start.2
  441.1 9.1 %fusion.4 = f32[4096,256]{1,0:T(8,128)S(1)} fusion(f32[256,4096]{1,0:T(8,128)} %copy-done, f32[128,256]{1,0:T(8,128)S(1)} %fusion.25, f32[128,256]{1,0:T(8,128)S(1)} %fusion.20), kind=kOutput, calls=%fused_computation.13 | convolution fusion | flops 3221291008 | bytes 8650752 | tf_op jit(solution)/shard_map/dot_general | solution.py:8
  450.3 0.0 copy-start.1
  450.3 1.9 copy-done.1
  452.2 0.0 copy-done.2
  452.2 7.5 %fusion.46 = f32[256,128]{1,0:T(8,128)} fusion(f32[4096,256]{1,0:T(8,128)S(1)} %fusion.4, f32[4096,128]{1,0:T(8,128)S(1)} %copy-done.2), kind=kOutput, calls=%fused_computation.78 | convolution fusion | flops 1610612736 | bytes 6422528 | tf_op jit(solution)/shard_map/dot_general | solution.py:12
  459.7 0.0 all-reduce.9.cloned.1.call-update
  459.8 1.2 fusion.14
  461.0 137.4 %all-reduce.9.cloned.1.call-done = f32[256,128]{1,0:T(8,128)} async-done(((f32[256,128]{1,0:T(8,128)}), f32[256,128]{1,0:T(8,128)}) %all-reduce.9.cloned.1.call-update) | async-done | bytes 131088 | tf_op jit(solution)/shard_map/psum | solution.py:37
  598.4 0.0 copy-start.3
  598.4 7.0 %convolution_subtract_fusion = f32[4096,128]{1,0:T(8,128)} fusion(f32[4096,128]{1,0:T(8,128)S(1)} %copy-done.2, f32[4096,256]{1,0:T(8,128)} %copy-done.1, f32[256,128]{1,0:T(8,128)} %all-reduce.9.cloned.1.call-done), kind=kOutput, calls=%fused_computation.4 | convolution fusion | flops 1611137024 | bytes 8519680 | tf_op jit(solution)/shard_map/dot_general | solution.py:8
  605.4 0.0 copy-done.3
  605.4 0.7 copy.36
  (18 shorter events, 0.3 us)
Async XLA Ops:
  7.2 154.5 %all-reduce.5.cloned.1.call-start = ((), (), s32[]{:S(2)}) async-start(), calls=%async_computation | async-start | bytes 524288 | tf_op jit(solution)/shard_map/psum | solution.py:22
  18.1 359.4 %all-reduce.7.cloned.1.call-start = ((), (), s32[]{:S(2)}) async-start(), calls=%async_computation.1 | async-start | bytes 524288 | tf_op jit(solution)/shard_map/psum | solution.py:22
  230.2 1.9 copy-start
  236.4 362.0 %all-reduce.9.cloned.1.call-start = ((), (), s32[]{:S(2)}) async-start(), calls=%async_computation.2 | async-start | bytes 262144 | tf_op jit(solution)/shard_map/psum | solution.py:37
  441.1 11.1 %copy-start.2 = (f32[4096,128]{1,0:T(8,128)S(1)}, f32[4096,128]{1,0:T(8,128)}, u32[]{:S(2)}) copy-start(f32[4096,128]{1,0:T(8,128)} %param.6) | copy-start | bytes 6291460
  450.3 1.9 copy-start.1
  598.4 7.0 %copy-start.3 = (f32[256,128]{1,0:T(8,128)S(1)}, f32[256,128]{1,0:T(8,128)}, u32[]{:S(2)}) copy-start(f32[256,128]{1,0:T(8,128)} %all-reduce.9.cloned.1.call-done) | copy-start | bytes 393220
Sparse Core Ops, SparseCore 0:
  18.2 143.3 all-reduce.4
  236.5 140.9 all-reduce.6
  459.9 138.4 all-reduce.8
where the time goes:
time: 621 us; the launch traced here: 613 us
  waiting for transfers between devices  422 us (68%)
  other arithmetic  110 us (18%)
  matrix products  48.1 us (8%)
  between operations  16.8 us (3%)
  local copies, waits for them, and re-layouts  14.8 us (2%)
    psum x2, waiting for transfers between devices, gram_of(): return lax.psum(inner(left, left), 'rows')  284 us
    psum x1, waiting for transfers between devices, on_device(): projected = lax.psum(inner(basis, trailing), 'rows')  137 us
    another operation x13, other arithmetic, lower_inverse(): lower = jnp.linalg.cholesky(gram)  68.6 us
    another operation x5, other arithmetic, lower_inverse(): lax.linalg.triangular_solve(lower, identity, left_side=True, lower=True)  39.4 us
    dot_general x4, matrix products, product(): jnp.dot(left, right, precision=lax.Precision.HIGHEST, preferred_element_t...  22.8 us
    dot_general x3, matrix products, inner(): lax.dot_general(left, right, (((0,), (0,)), ((), ())), precision=lax.Prec...  22.6 us
  transfers between devices with their start and end apart: 3, of which 3 were waited for; matrix products, arithmetic and copies ran while one was open for 0% of the time, Pallas kernels for 0%

commit v1 on v0

v1 whole, which is shorter than its diff:
```python
import jax
import jax.numpy as jnp
from jax import lax
from jax.experimental import pallas as pl
from jax.experimental.pallas import tpu as pltpu
from jax.sharding import PartitionSpec as P

F32 = jnp.float32
BF16 = jnp.bfloat16
N = 256
H = 128
RING = 32
VMEM = 48 * 1024 * 1024


def dot_t(a, b):
    return lax.dot_general(a, b, (((0,), (0,)), ((), ())), preferred_element_type=F32)


def dot_n(a, b):
    return lax.dot_general(a, b, (((1,), (0,)), ((), ())), preferred_element_type=F32)


def dot_r(a, b):
    return lax.dot_general(a, b, (((1,), (1,)), ((), ())), preferred_element_type=F32)


def split3(x):
    one = x.astype(BF16)
    rest = x - one.astype(F32)
    two = rest.astype(BF16)
    three = (rest - two.astype(F32)).astype(BF16)
    return one, two, three


def product6(dot, a, b):
    a1, a2, a3 = split3(a)
    b1, b2, b3 = split3(b)
    small = (dot(a1, b3) + dot(a3, b1)) + dot(a2, b2)
    return dot(a1, b1) + ((dot(a1, b2) + dot(a2, b1)) + small)


def power_near(x):
    big = x * F32(2.0**23 + 1.0)
    return big - (big - x)


def grid_split(x, bits):
    top = jnp.max(jnp.abs(x), axis=0, keepdims=True)
    magic = power_near(top) * F32(1.5 * 2.0 ** (23 - bits))
    coarse = (x + magic) - magic
    rest = x - coarse
    two = rest.astype(BF16)
    three = (rest - two.astype(F32)).astype(BF16)
    return coarse.astype(BF16), two, three


def two_sum(a, b):
    s = a + b
    t = s - a
    return s, (a - (s - t)) + (b - t)


def gram_kernel(panel_ref, trailing_ref, out_ref, hi, lo, cross, proj):
    step = pl.program_id(0)

    @pl.when(step == 0)
    def _():
        hi[...] = jnp.zeros_like(hi)
        lo[...] = jnp.zeros_like(lo)
        cross[...] = jnp.zeros_like(cross)
        proj[...] = jnp.zeros_like(proj)

    a1, a2, a3 = grid_split(panel_ref[...], 6)
    t1, t2, t3 = split3(trailing_ref[...])
    exact = dot_t(a1, a1)
    half = a2 * BF16(0.5)
    cross[...] += (dot_t(a1, a2) + dot_t(a1, a3)) + (dot_t(a2, half) + dot_t(a2, a3))
    proj[...] += dot_t(a1, t1) + (
        (dot_t(a1, t2) + dot_t(a2, t1)) + ((dot_t(a1, t3) + dot_t(a3, t1)) + dot_t(a2, t2))
    )
    s, e = two_sum(hi[...], exact)
    hi[...] = s
    lo[...] += e

    @pl.when(step == pl.num_programs(0) - 1)
    def _():
        v = cross[...]
        c = v + v.T
        s, e = two_sum(hi[...], c)
        hi[...] = s
        lo[...] += e
        for d in range(RING):
            for k in range(3):
                r0 = 12 * d + 4 * k
                rows = slice(r0 % H + (0 if r0 < H else H), r0 % H + (0 if r0 < H else H) + 4)
                cols = slice(0, H) if r0 < 2 * H else slice(H, N)
                out_ref[d, 4 * k : 4 * k + 4, :] = hi[rows, cols]
                out_ref[d, 12 + 4 * k : 16 + 4 * k, :] = lo[rows, cols]
            out_ref[d, 24:32, :] = proj[8 * d : 8 * d + 8, :]


def gram(panel, trailing):
    rows = panel.shape[0]
    chunk = 1024
    return pl.pallas_call(
        gram_kernel,
        grid=(rows // chunk,),
        in_specs=[
            pl.BlockSpec((chunk, N), lambda i: (i, 0)),
            pl.BlockSpec((chunk, H), lambda i: (i, 0)),
        ],
        out_specs=pl.BlockSpec((RING, 32, H), lambda i: (0, 0, 0)),
        out_shape=jax.ShapeDtypeStruct((RING, 32, H), F32),
        scratch_shapes=[
            pltpu.VMEM((N, N), F32),
            pltpu.VMEM((N, N), F32),
            pltpu.VMEM((N, N), F32),
            pltpu.VMEM((N, H), F32),
        ],
        compiler_params=pltpu.CompilerParams(vmem_limit_bytes=VMEM),
        name="products",
    )(panel, trailing)


def sum_kernel(in_ref, out_ref):
    parts = [(in_ref[d], None) for d in range(RING)]
    while len(parts) > 1:
        merged = []
        for (a, ea), (b, eb) in zip(parts[::2], parts[1::2]):
            s, e = two_sum(a, b)
            if ea is not None:
                e = e + (ea + eb)
            merged.append((s, e))
        parts = merged
    s, e = parts[0]
    hi, lo = two_sum(s[0:12], s[12:24] + e[0:12])
    out = jnp.concatenate([hi, lo, s[24:32] + e[24:32]], axis=0)
    out_ref[...] = jnp.broadcast_to(out[None], (RING, 32, H))


def sum_parts(received):
    return pl.pallas_call(
        sum_kernel,
        out_shape=jax.ShapeDtypeStruct((RING, 32, H), F32),
        compiler_params=pltpu.CompilerParams(vmem_limit_bytes=VMEM),
        name="sum_parts",
    )(received)


def factor_kernel(in_ref, factor_ref, proj_ref, coef_ref, hi, lo, c_ref, g, b):
    for d in range(RING):
        for k in range(3):
            r0 = 12 * d + 4 * k
            hi[r0 : r0 + 4, :] = in_ref[d, 4 * k : 4 * k + 4, :]
            lo[r0 : r0 + 4, :] = in_ref[d, 12 + 4 * k : 16 + 4 * k, :]
        c_ref[8 * d : 8 * d + 8, :] = in_ref[d, 24:32, :]
    g[0:H, 0:H] = hi[0:H, :]
    g[0:H, H:N] = hi[H : 2 * H, :].T
    g[H:N, 0:H] = jnp.zeros((H, H), F32)
    g[H:N, H:N] = hi[2 * H : 3 * H, :]
    row = lax.broadcasted_iota(jnp.int32, (N, N), 0)
    col = lax.broadcasted_iota(jnp.int32, (N, N), 1)
    b[...] = jnp.where(row == col, F32(1.0), F32(0.0))
    sub = lax.broadcasted_iota(jnp.int32, (8, H), 0)

    blocks = N // 8
    window = 3
    for t in range(blocks):
        groups = [(g, 0), (g, 1), (b, 0)] if t < blocks // 2 else [(g, 1), (b, 0), (b, 1)]
        wide = [w for w in range(window) if t + w < blocks]
        rows = [
            [ref[8 * (t + w) : 8 * (t + w) + 8, H * q : H * q + H] for ref, q in groups] for w in wide
        ]
        lane = (8 * t) % H
        if t < blocks // 2:
            pass
        x = [[None] * 8 for _ in wide]
        for w in wide:
            for k in range(8):
                if t < blocks // 2 and t + w >= blocks // 2:
                    piece = rows[0][1][:, (8 * (t + w)) % H : (8 * (t + w)) % H + 8].T
                    x[w][k] = jnp.broadcast_to(piece[:, k : k + 1], (8, H))
                else:
                    x[w][k] = jnp.broadcast_to(rows[w][0][:, lane + k : lane + k + 1], (8, H))
        for k in range(8):
            rs = lax.rsqrt(jnp.broadcast_to(x[0][k][k : k + 1, :], (8, H)))
            u = [x[w][k] * rs for w in wide]
            line = [jnp.broadcast_to(rows[0][q][k : k + 1, :], (8, H)) * rs for q in range(3)]
            for j in range(k + 1, 8):
                f = jnp.broadcast_to(u[0][j : j + 1, :], (8, H))
                for w in wide:
                    x[w][j] = x[w][j] - u[w] * f
            below = jnp.where(sub > k, u[0], F32(0.0))
            for q in range(3):
                rows[0][q] = jnp.where(sub == k, line[q], rows[0][q] - below * line[q])
                for w in wide[1:]:
                    rows[w][q] = rows[w][q] - u[w] * line[q]
        for w in wide:
            for q, (ref, p) in enumerate(groups):
                ref[8 * (t + w) : 8 * (t + w) + 8, H * p : H * p + H] = rows[w][q]
        first = 8 * (t + window)
        if first < N:
            u = jnp.concatenate(rows[0], axis=1)
            u1 = u.astype(BF16).astype(F32)
            r = u - u1
            u2 = r.astype(BF16).astype(F32)
            u3 = r - u2
            left = jnp.concatenate([u1, u1, u2, u1, u2, u3], axis=0).astype(BF16)
            right = jnp.concatenate([u1, u2, u1, u3, u2, u1], axis=0).astype(BF16)
            for half in range(2):
                lo_row, hi_row = max(first, H * half), H * half + H
                if lo_row >= hi_row:
                    continue
                q = [i for i, (ref, p) in enumerate(groups) if ref is g and p == half][0]
                change = dot_t(left[:, H * q : H * q + H], right)
                for i, (ref, p) in enumerate(groups):
                    if ref is g and p < half:
                        continue
                    ref[lo_row:hi_row, H * p : H * p + H] -= change[
                        lo_row - H * half :, H * i : H * i + H
                    ]

    upper = jnp.where(row <= col, g[...], F32(0.0))
    inverse = jnp.where(row >= col, b[...], F32(0.0))
    u1, u2, u3 = grid_split(upper, 7)
    exact = dot_t(u1, u1)
    v = (dot_t(u1, u2) + dot_t(u1, u3)) + (dot_t(u2, u2 * BF16(0.5)) + dot_t(u2, u3))
    v = v + v.T

    def left_of(ref, other):
        return (ref[0:H, :] - other[0:H, 0:H], ref[H : 2 * H, :] - other[H:N, 0:H], ref[2 * H : 3 * H, :] - other[H:N, H:N])

    d00, d10, d11 = left_of(hi, exact)
    d00 = (d00 + lo[0:H, :]) - v[0:H, 0:H]
    d10 = (d10 + lo[H : 2 * H, :]) - v[H:N, 0:H]
    d11 = (d11 + lo[2 * H : 3 * H, :]) - v[H:N, H:N]
    d = jnp.concatenate(
        [jnp.concatenate([d00, d10.T], axis=1), jnp.concatenate([d10, d11], axis=1)], axis=0
    )
    e = product6(dot_r, product6(dot_n, inverse, d), inverse)
    scale = jnp.where(row > col, F32(1.0), jnp.where(row == col, F32(0.5), F32(0.0)))
    x = e * scale

    def again(state):
        old, _, count = state
        new = (e - product6(dot_r, old, old)) * scale
        return new, jnp.max(jnp.abs(new - old)), count + 1

    x, _, _ = lax.while_loop(
        lambda s: jnp.logical_and(s[1] > F32(1e-6), s[2] < 20), again, (x, F32(1.0), jnp.int32(0))
    )
    factor_ref[...] = upper + product6(dot_t, x, upper)
    x2 = product6(dot_n, x, x)
    x4 = product6(dot_n, x2, x2)
    w = inverse - product6(dot_n, x, inverse)
    w = w + product6(dot_n, x2, w)
    w = w + product6(dot_n, x4, w)
    p = product6(dot_n, w, c_ref[...])
    proj_ref[...] = p
    coef_ref[...] = product6(dot_t, w, p)


def factor(gathered):
    return pl.pallas_call(
        factor_kernel,
        out_shape=(
            jax.ShapeDtypeStruct((N, N), F32),
            jax.ShapeDtypeStruct((N, H), F32),
            jax.ShapeDtypeStruct((N, H), F32),
        ),
        scratch_shapes=[
            pltpu.VMEM((3 * H, H), F32),
            pltpu.VMEM((3 * H, H), F32),
            pltpu.VMEM((N, H), F32),
            pltpu.VMEM((N, N), F32),
            pltpu.VMEM((N, N), F32),
        ],
        compiler_params=pltpu.CompilerParams(vmem_limit_bytes=VMEM),
        name="factor",
    )(gathered)


def remainder_kernel(panel_ref, trailing_ref, coef_ref, out_ref):
    out_ref[...] = trailing_ref[...] - product6(dot_n, panel_ref[...], coef_ref[...])


def remainder_of(panel, trailing, coef):
    rows = panel.shape[0]
    chunk = 512
    return pl.pallas_call(
        remainder_kernel,
        grid=(rows // chunk,),
        in_specs=[
            pl.BlockSpec((chunk, N), lambda i: (i, 0)),
            pl.BlockSpec((chunk, H), lambda i: (i, 0)),
            pl.BlockSpec((N, H), lambda i: (0, 0)),
        ],
        out_specs=pl.BlockSpec((chunk, H), lambda i: (i, 0)),
        out_shape=jax.ShapeDtypeStruct((rows, H), F32),
        compiler_params=pltpu.CompilerParams(vmem_limit_bytes=VMEM),
        name="remainder",
    )(panel, trailing, coef)


def on_device(panel, trailing):
    sent = gram(panel, trailing)
    received = lax.all_to_all(sent, "rows", 0, 0, tiled=True)
    summed = sum_parts(received)
    gathered = lax.all_to_all(summed, "rows", 0, 0, tiled=True)
    factor_r, projected, coef = factor(gathered)
    return factor_r, projected, remainder_of(panel, trailing, coef)


def solution(mesh):
    return jax.shard_map(
        on_device,
        mesh=mesh,
        in_specs=(P("rows", None), P("rows", "cols")),
        out_specs=(P(), P(None, "cols"), P("rows", "cols")),
        check_vma=False,
    )
```

time: 621 us -> 83.1 us (0.13)
  the two profiles are of different devices: /device:TPU:1 before, /device:TPU:16 now
where the time goes in v1:
time: 83.1 us; the launch traced here: 82.7 us
  blocking collectives  50.4 us (61%)
  Pallas kernels  30.1 us (36%)
  local copies, waits for them, and re-layouts  1.59 us (2%)
    all_to_all x1, blocking collectives, on_device(): received = lax.all_to_all(sent, 'rows', 0, 0, tiled=True)  29 us
    all_to_all x1, blocking collectives, on_device(): gathered = lax.all_to_all(summed, 'rows', 0, 0, tiled=True)  21.4 us
    pallas_call x1, Pallas kernels, factor(): pl.pallas_call(factor_kernel, out_shape=(jax.ShapeDtypeStruct((N, N), F32...  12.7 us
    pallas_call x1, Pallas kernels, gram(): pl.pallas_call(gram_kernel, grid=(rows // chunk,), in_specs=[pl.BlockSpec...  8.95 us
    pallas_call x1, Pallas kernels, remainder_of(): pl.pallas_call(remainder_kernel, grid=(rows // chunk,), in_specs=[pl.Bloc...  8.27 us

profile of v1, /device:TPU:16, one launch (start us, length us, event | category | flops | bytes accessed | tf_op | source)
XLA Modules:
  0.0 82.7 jit_solution(3856483945619175441)
XLA Ops:
  0.6 0.0 copy-start
  0.6 1.6 %copy-done = f32[4096,128]{1,0:T(8,128)S(1)} copy-done((f32[4096,128]{1,0:T(8,128)S(1)}, f32[4096,128]{1,0:T(8,128)}, u32[]{:S(2)}) %copy-start) | copy-done | bytes 2097176
  2.2 8.9 %products.1 = f32[32,32,128]{2,1,0:T(8,128)S(1)} custom-call(f32[4096,256]{1,0:T(8,128)} %panel_ref.3, f32[4096,128]{1,0:T(8,128)S(1)} %copy-done), custom_call_target="tpu_custom_call" | custom-call | tf_op jit(solution)/shard_map/products/pallas_call | solution.py:106
  11.2 0.0 copy-start.1
  11.2 29.0 %all_to_all.10.in_ref = f32[32,32,128]{2,1,0:T(8,128)S(1)} all-to-all(f32[32,32,128]{2,1,0:T(8,128)S(1)} %products.1), channel_id=1, replica_groups=mesh['rows'=32,'cols'=8] {'rows'}, dimensions={0} | all-to-all | bytes 1048576 | tf_op jit(solution)/shard_map/all_to_all | solution.py:308
  40.1 0.1 sum_parts.1
  40.3 21.4 %all_to_all.11.in_ref = f32[32,32,128]{2,1,0:T(8,128)S(1)} all-to-all(f32[32,32,128]{2,1,0:T(8,128)S(1)} %sum_parts.1), channel_id=1, replica_groups=mesh['rows'=32,'cols'=8] {'rows'}, dimensions={0} | all-to-all | bytes 1048576 | tf_op jit(solution)/shard_map/all_to_all | solution.py:310
  61.7 12.7 %factor.1 = (f32[256,256]{1,0:T(8,128)}, f32[256,128]{1,0:T(8,128)}, f32[256,128]{1,0:T(8,128)S(1)}) custom-call(f32[32,32,128]{2,1,0:T(8,128)S(1)} %all_to_all.11.in_ref), custom_call_target="tpu_custom_call" | custom-call | tf_op jit(solution)/shard_map/factor/pallas_call | solution.py:265
  74.4 0.0 copy-done.1
  74.4 8.3 %remainder.1 = f32[4096,128]{1,0:T(8,128)} custom-call(f32[4096,256]{1,0:T(8,128)} %panel_ref.3, f32[4096,128]{1,0:T(8,128)S(1)} %copy-done.1, f32[256,128]{1,0:T(8,128)S(1)} %get-tuple-element.8.coef_ref), custom_call_target="tpu_custom_call" | custom-call | tf_op jit(solution)/shard_map/remainder/pallas_call | solution.py:291
Async XLA Ops:
  0.6 1.6 %copy-start = (f32[4096,128]{1,0:T(8,128)S(1)}, f32[4096,128]{1,0:T(8,128)}, u32[]{:S(2)}) copy-start(f32[4096,128]{1,0:T(8,128)} %trailing_ref.3) | copy-start | bytes 6291460
  11.2 63.2 %copy-start.1 = (f32[4096,128]{1,0:T(8,128)S(1)}, f32[4096,128]{1,0:T(8,128)}, u32[]{:S(2)}) copy-start(f32[4096,128]{1,0:T(8,128)} %trailing_ref.3) | copy-start | bytes 6291460

commit v2 on v0

v2 whole, which is shorter than its diff:
```python
import jax
import jax.numpy as jnp
from jax import lax
from jax.experimental import pallas as pl
from jax.experimental.pallas import tpu as pltpu
from jax.sharding import PartitionSpec as P

F32 = jnp.float32
BF16 = jnp.bfloat16
N = 256
H = 128
RING = 32
VMEM = 48 * 1024 * 1024


def dot_t(a, b):
    return lax.dot_general(a, b, (((0,), (0,)), ((), ())), preferred_element_type=F32)


def dot_n(a, b):
    return lax.dot_general(a, b, (((1,), (0,)), ((), ())), preferred_element_type=F32)


def dot_r(a, b):
    return lax.dot_general(a, b, (((1,), (1,)), ((), ())), preferred_element_type=F32)


def split3(x):
    one = x.astype(BF16)
    rest = x - one.astype(F32)
    two = rest.astype(BF16)
    three = (rest - two.astype(F32)).astype(BF16)
    return one, two, three


def product6s(dot, a, b):
    small = (dot(a[0], b[2]) + dot(a[2], b[0])) + dot(a[1], b[1])
    return dot(a[0], b[0]) + ((dot(a[0], b[1]) + dot(a[1], b[0])) + small)


def product6(dot, a, b):
    return product6s(dot, split3(a), split3(b))


def power_near(x):
    big = x * F32(2.0**23 + 1.0)
    return big - (big - x)


def grid_split(x, bits):
    top = jnp.max(jnp.abs(x), axis=0, keepdims=True)
    magic = power_near(top) * F32(1.5 * 2.0 ** (23 - bits))
    coarse = (x + magic) - magic
    rest = x - coarse
    two = rest.astype(BF16)
    three = (rest - two.astype(F32)).astype(BF16)
    return coarse.astype(BF16), two, three


def two_sum(a, b):
    s = a + b
    t = s - a
    return s, (a - (s - t)) + (b - t)


CHUNK = 1024


def gram_kernel(core_ref, panel_hbm, trailing_hbm, out_ref, panel, trailing, sems):
    height = panel.shape[0]
    chunks = height // CHUNK

    def copies(i, start, size):
        rows = pl.ds(start, size)
        return (
            pltpu.make_async_copy(panel_hbm.at[rows], panel.at[rows], sems.at[0, i]),
            pltpu.make_async_copy(trailing_hbm.at[rows], trailing.at[rows], sems.at[1, i]),
        )

    first = copies(0, 0, CHUNK)
    later = copies(1, CHUNK, height - CHUNK)
    for copy in first + later:
        copy.start()
    first_core = core_ref[0] == 0

    def split(i):
        rows = slice(i * CHUNK, i * CHUNK + CHUNK)
        a = grid_split(panel[rows, :], 6)
        t = split3(trailing[rows, :])
        b = [
            jnp.concatenate([jnp.where(first_core, x[:, 0:H], x[:, H:N]), y], axis=1)
            for x, y in zip(a, t)
        ]
        return a, b

    for copy in first:
        copy.wait()
    held = split(0)
    for copy in later:
        copy.wait()
    hi = lo = rest = mixed = jnp.zeros((N, N), F32)
    for i in range(chunks):
        (a1, a2, a3), (b1, b2, b3) = held
        if i + 1 < chunks:
            held = split(i + 1)
        one = dot_t(a1, jnp.concatenate([b1, b2, b3], axis=1))
        two = dot_t(a2, jnp.concatenate([b1, b2, a3], axis=1))
        rest = rest + (one[:, N : 2 * N] + one[:, 2 * N :] + (two[:, 0:N] + two[:, N : 2 * N] + dot_t(a3, b1)))
        mixed = mixed + two[:, 2 * N :]
        hi, e = two_sum(hi, one[:, 0:N])
        lo = lo + e
    mixed = mixed + mixed.T
    s, e = two_sum(hi[:, 0:H], rest[:, 0:H] + jnp.where(first_core, mixed[:, 0:H], mixed[:, H:N]))
    out_ref[:, 0:8, :] = s.reshape(RING, 8, H)
    out_ref[:, 8:16, :] = (lo[:, 0:H] + e).reshape(RING, 8, H)
    out_ref[:, 16:24, :] = (hi[:, H:N] + (lo[:, H:N] + rest[:, H:N])).reshape(RING, 8, H)


def gram(core, panel, trailing):
    rows = panel.shape[0]
    return pl.pallas_call(
        gram_kernel,
        in_specs=[
            pl.BlockSpec(memory_space=pltpu.SMEM),
            pl.BlockSpec(memory_space=pl.ANY),
            pl.BlockSpec(memory_space=pl.ANY),
        ],
        out_specs=pl.BlockSpec(memory_space=pltpu.VMEM),
        out_shape=jax.ShapeDtypeStruct((RING, 24, H), F32),
        scratch_shapes=[
            pltpu.VMEM((rows, N), F32),
            pltpu.VMEM((rows, H), F32),
            pltpu.SemaphoreType.DMA((2, 2)),
        ],
        compiler_params=pltpu.CompilerParams(vmem_limit_bytes=60 * 1024 * 1024),
        name="products",
    )(core, panel, trailing)


def sum_kernel(in_ref, out_ref):
    parts = [(in_ref[d], None) for d in range(RING)]
    while len(parts) > 1:
        merged = []
        for (a, ea), (b, eb) in zip(parts[::2], parts[1::2]):
            s, e = two_sum(a, b)
            if ea is not None:
                e = e + (ea + eb)
            merged.append((s, e))
        parts = merged
    s, e = parts[0]
    hi, lo = two_sum(s[0:8], s[8:16] + e[0:8])
    out = jnp.concatenate([hi, lo, s[16:24] + e[16:24]], axis=0)
    out_ref[...] = jnp.broadcast_to(out[None], (RING, 24, H))


def sum_parts(received):
    return pl.pallas_call(
        sum_kernel,
        out_shape=jax.ShapeDtypeStruct((RING, 24, H), F32),
        compiler_params=pltpu.CompilerParams(vmem_limit_bytes=VMEM),
        name="sum_parts",
    )(received)


def eliminate(g, b):
    sub = lax.broadcasted_iota(jnp.int32, (8, H), 0)
    group, slack, depth = 2, 2, 1
    blocks = N // 8
    half = blocks // 2

    def groups_of(t):
        return [(g, 0), (g, 1), (b, 0)] if t < half else [(g, 1), (b, 0), (b, 1)]

    def spread(rows, groups, column):
        q = [i for i, (ref, p) in enumerate(groups) if ref is g and p == column // H][0]
        lane = column % H
        return jnp.broadcast_to(rows[q][:, lane : lane + 1], (8, H))

    def over(x, j):
        return jnp.broadcast_to(x[j : j + 1, :], (8, H))

    x, done = [], []
    for t in range(blocks):
        window = group - t % group + slack
        groups = groups_of(t)
        wide = [w for w in range(window) if t + w < blocks]
        rows = [
            [ref[8 * (t + w) : 8 * (t + w) + 8, H * p : H * p + H] for ref, p in groups] for w in wide
        ]
        for w in wide[len(x) :]:
            x.append([spread(rows[w], groups, 8 * t + k) for k in range(8)])
        near = wide[1 : 1 + depth]
        ahead = [None] + [[spread(rows[w], groups, 8 * t + 8 + k) for k in range(8)] for w in near]
        d = over(x[0][0], 0)
        scale = jnp.zeros((8, H), F32)
        for k in range(8):
            r = pltpu.reciprocal(d, approx=True)
            scale = jnp.where(sub == k, lax.rsqrt(d), scale)
            if k < 7:
                corner = over(x[0][k], k + 1)
                d = over(x[0][k + 1], k + 1) - (corner * corner) * r
            u = [x[w][k] * r for w in wide]
            for j in range(k + 1, 8):
                f = over(u[0], j)
                for w in wide:
                    x[w][j] = x[w][j] - x[w][k] * f
            if near:
                for j in range(8):
                    f = over(u[1], j)
                    for w in near:
                        ahead[w][j] = ahead[w][j] - x[w][k] * f
            u[0] = jnp.where(sub > k, u[0], F32(0.0))
            for q in range(3):
                line = over(rows[0][q], k)
                for w in wide:
                    rows[w][q] = rows[w][q] - u[w] * line
        rows[0] = [piece * scale for piece in rows[0]]
        for w in wide:
            for q, (ref, p) in enumerate(groups):
                ref[8 * (t + w) : 8 * (t + w) + 8, H * p : H * p + H] = rows[w][q]
        x = ahead[1:]
        done.append(jnp.concatenate(rows[0], axis=1))
        first = 8 * (t + 1 + slack)
        if t % group < group - 1:
            continue
        if first < N:
            u1, u2, u3 = split3(jnp.concatenate(done, axis=0))
            left = jnp.concatenate([u1, u1, u2, u1, u2, u3], axis=0)
            right = jnp.concatenate([u1, u2, u1, u3, u2, u1], axis=0)
            for part in range(2):
                top, end = max(first, H * part), H * part + H
                if top >= end:
                    continue
                q = [i for i, (ref, p) in enumerate(groups) if ref is g and p == part][0]
                change = dot_t(left[:, H * q : H * q + H], right)
                for i, (ref, p) in enumerate(groups):
                    stop = min(end, H + 8 * (group + slack)) if ref is g and p < part else end
                    if top < stop:
                        ref[top:stop, H * p : H * p + H] -= change[
                            top - H * part : stop - H * part, H * i : H * i + H
                        ]
        done = []


def product3(dot, a, b):
    return dot(a[0], b[0]) + (dot(a[0], b[1]) + dot(a[1], b[0]))


def split2(x):
    one = x.astype(BF16)
    return one, (x - one.astype(F32)).astype(BF16)


STRIP = 512


def factor_kernel(
    core_ref, own_ref, other_ref, panel_hbm, trailing_hbm, factor_hbm, proj_hbm, rest_hbm,
    panel, trailing, rest, factor_ref, proj_ref, hi, lo, g, b, xs, qs, in_sems, out_sems,
):
    loads = (
        pltpu.make_async_copy(panel_hbm, panel, in_sems.at[0]),
        pltpu.make_async_copy(trailing_hbm, trailing, in_sems.at[1]),
    )
    for copy in loads:
        copy.start()
    first_core = core_ref[0] == 0
    for ref, at in ((hi, 0), (lo, 8)):
        mine = own_ref[:, at : at + 8, :].reshape(N, H)
        theirs = other_ref[:, at : at + 8, :].reshape(N, H)
        ref[:, 0:H] = jnp.where(first_core, mine, theirs)
        ref[:, H:N] = jnp.where(first_core, theirs, mine)
    c = own_ref[:, 16:24, :].reshape(N, H)
    g[...] = hi[...]
    row = lax.broadcasted_iota(jnp.int32, (N, N), 0)
    col = lax.broadcasted_iota(jnp.int32, (N, N), 1)
    b[...] = jnp.where(row == col, F32(1.0), F32(0.0))
    eliminate(g, b)

    upper = jnp.where(row <= col, g[...], F32(0.0))
    inverse = jnp.where(row >= col, b[...], F32(0.0))
    w1, w2, w3 = split3(inverse)
    y = product6s(dot_n, (w1, w2, w3), split3(c))
    u1, u2, u3 = grid_split(upper, 7)
    exact = dot_t(u1, u1)
    v = (dot_t(u1, u2) + dot_t(u1, u3)) + (dot_t(u2, u2 * BF16(0.5)) + dot_t(u2, u3))
    d = ((hi[...] - exact) + lo[...]) - (v + v.T)
    f = product3(dot_n, (w1, w2), split2(d))
    e = product3(dot_r, split2(f), (w1, w2))
    size = jnp.max(jnp.sum(jnp.abs(e), axis=0, keepdims=True))
    lower = jnp.where(row > col, F32(1.0), jnp.where(row == col, F32(0.5), F32(0.0)))
    es = split2(e)
    ee = product3(dot_n, es, es)
    q = y - product3(dot_n, es, split2(y))
    q = q + product3(dot_n, split2(ee), split2(q))
    x = e * lower
    xb = split2(x)
    x = (e - product3(dot_r, xb, xb)) * lower
    xs[...] = x
    qs[...] = q

    @pl.when(jnp.logical_not(size < F32(0.03)))
    def _():
        def again(state):
            old, _, count = state
            new = (e - product6(dot_r, old, old)) * lower
            return new, jnp.max(jnp.abs(new - old)), count + 1

        x, _, _ = lax.while_loop(
            lambda s: jnp.logical_and(s[1] > F32(1e-6), s[2] < 60), again, (xs[...], F32(1.0), jnp.int32(0))
        )
        q, power = y, -e
        for _ in range(6):
            q = q + product6(dot_n, power, q)
            power = product6(dot_n, power, power)
        xs[...] = x
        qs[...] = q

    q = qs[...]
    xb = split2(xs[...])
    z1, z2, z3 = split3(product6s(dot_t, (w1, w2, w3), split3(q)))
    proj_ref[...] = q + product3(dot_t, xb, split2(q))
    factor_ref[...] = upper + product3(dot_t, xb, split2(upper))
    strips = panel.shape[0] // STRIP
    stores = [
        pltpu.make_async_copy(factor_ref, factor_hbm, out_sems.at[strips]),
        pltpu.make_async_copy(proj_ref, proj_hbm, out_sems.at[strips + 1]),
    ]
    for copy in stores:
        copy.start()
    zero = jnp.zeros_like(z1)
    right = jnp.concatenate(
        [
            jnp.concatenate(pair, axis=1)
            for pair in ((z1, z2), (z3, zero), (z1, z2), (z1, zero))
        ],
        axis=0,
    )
    for copy in loads:
        copy.wait()
    for i in range(strips):
        rows = slice(i * STRIP, i * STRIP + STRIP)
        a1, a2, a3 = split3(panel[rows, :])
        both = dot_n(jnp.concatenate([a1, a1, a2, a3], axis=1), right)
        rest[rows, :] = trailing[rows, :] - (both[:, 0:H] + both[:, H:N])
        store = pltpu.make_async_copy(rest.at[rows], rest_hbm.at[rows], out_sems.at[i])
        store.start()
        stores.append(store)
    for copy in stores:
        copy.wait()


def factor(core, own, other, panel, trailing):
    rows = panel.shape[0]
    return pl.pallas_call(
        factor_kernel,
        in_specs=[pl.BlockSpec(memory_space=pltpu.SMEM)]
        + [pl.BlockSpec(memory_space=pltpu.VMEM)] * 2
        + [pl.BlockSpec(memory_space=pl.ANY)] * 2,
        out_specs=[pl.BlockSpec(memory_space=pl.ANY)] * 3,
        out_shape=(
            jax.ShapeDtypeStruct((N, N), F32),
            jax.ShapeDtypeStruct((N, H), F32),
            jax.ShapeDtypeStruct((rows, H), F32),
        ),
        scratch_shapes=[
            pltpu.VMEM((rows, N), F32),
            pltpu.VMEM((rows, H), F32),
            pltpu.VMEM((rows, H), F32),
            pltpu.VMEM((N, N), F32),
            pltpu.VMEM((N, H), F32),
            pltpu.VMEM((N, N), F32),
            pltpu.VMEM((N, N), F32),
            pltpu.VMEM((N, N), F32),
            pltpu.VMEM((N, N), F32),
            pltpu.VMEM((N, N), F32),
            pltpu.VMEM((N, H), F32),
            pltpu.SemaphoreType.DMA((2,)),
            pltpu.SemaphoreType.DMA((rows // STRIP + 2,)),
        ],
        compiler_params=pltpu.CompilerParams(vmem_limit_bytes=VMEM),
        name="factor",
    )(core, own, other, panel, trailing)


def on_device(panel, trailing):
    core = lax.axis_index("cols").astype(jnp.int32).reshape(1) % 2
    sent = gram(core, panel, trailing)
    received = lax.all_to_all(sent, "rows", 0, 0, tiled=True)
    summed = sum_parts(received)
    own = lax.all_to_all(summed, "rows", 0, 0, tiled=True)
    other = lax.ppermute(own, "cols", [(j, j ^ 1) for j in range(lax.axis_size("cols"))])
    return tuple(factor(core, own, other, panel, trailing))


def solution(mesh):
    return jax.shard_map(
        on_device,
        mesh=mesh,
        in_specs=(P("rows", None), P("rows", "cols")),
        out_specs=(P(), P(None, "cols"), P("rows", "cols")),
        check_vma=False,
    )
```

time: 621 us -> 69.2 us (0.11); the launches traced: 613 us -> 68.9 us
  waiting for transfers between devices: 422 us -> 1.35 us
  other arithmetic: 110 us -> 0 us
  matrix products: 48.1 us -> 0 us
  blocking collectives: 0 us -> 43.5 us
  Pallas kernels: 0 us -> 19.9 us
  between operations: 16.8 us -> 0.82 us
  local copies, waits for them, and re-layouts: 14.8 us -> 0.01 us
    psum x3 -> x0, waiting for transfers between devices: 422 us -> none  [the longest x2 284 us: gram_of(): return lax.psum(inner(left, left), 'rows')]
    another operation x18 -> x0, other arithmetic: 108 us -> none  [the longest x13 68.6 us: lower_inverse(): lower = jnp.linalg.cholesky(gram)]
    dot_general x7 -> x0, matrix products: 45.4 us -> none  [the longest x4 22.8 us: product(): jnp.dot(left, right, precision=lax.Precision.HIGHEST, preferred_element_t...]
    all_to_all x0 -> x2, blocking collectives: none -> 43.5 us  [the longest x1 25.8 us: on_device(): received = lax.all_to_all(sent, 'rows', 0, 0, tiled=True)]
    pallas_call x0 -> x3, Pallas kernels: none -> 19.9 us  [the longest x1 11.4 us: factor(): pl.pallas_call(factor_kernel, in_specs=[pl.BlockSpec(memory_space=pltpu.S...]
    another operation x19 -> x0, local copies, waits for them, and re-layouts: 8.15 us -> none  [the longest x15 8.1 us: lower_inverse(): lax.linalg.triangular_solve(lower, identity, left_side=True, lower=True)]
  transfers between devices with their start and end apart: 3 -> 1, of which waited for: 3 -> 1; matrix products, arithmetic and copies ran while one was open for 0% -> 0% of each run, Pallas kernels for 0% -> 0%
where the time goes in v2:
time: 69.2 us; the launch traced here: 68.9 us
  blocking collectives  43.5 us (63%)
  Pallas kernels  19.9 us (29%)
  starting transfers between devices  3.34 us (5%)
  waiting for transfers between devices  1.35 us (2%)
  between operations  0.82 us (1%)
    all_to_all x1, blocking collectives, on_device(): received = lax.all_to_all(sent, 'rows', 0, 0, tiled=True)  25.8 us
    all_to_all x1, blocking collectives, on_device(): own = lax.all_to_all(summed, 'rows', 0, 0, tiled=True)  17.7 us
    pallas_call x1, Pallas kernels, factor(): pl.pallas_call(factor_kernel, in_specs=[pl.BlockSpec(memory_space=pltpu.S...  11.4 us
    pallas_call x1, Pallas kernels, gram(): pl.pallas_call(gram_kernel, in_specs=[pl.BlockSpec(memory_space=pltpu.SME...  8.46 us
    ppermute x1, starting transfers between devices, on_device(): lax.ppermute(own, 'cols', [(j, j ^ 1) for j in range(lax.axis_size('cols'...  3.34 us
  transfers between devices with their start and end apart: 1, of which 1 were waited for; matrix products, arithmetic and copies ran while one was open for 0% of the time, Pallas kernels for 0%

profile of v2, /device:TPU:1, one launch (start us, length us, event | category | flops | bytes accessed | tf_op | source)
XLA Modules:
  0.0 68.9 jit_solution(8202724557821764720)
XLA Ops:
  0.6 8.5 %products.1 = f32[32,24,128]{2,1,0:T(8,128)} custom-call(s32[1]{0:T(128)S(6)} %select_n.7.core_ref, f32[4096,256]{1,0:T(8,128)} %panel_hbm.3, f32[4096,128]{1,0:T(8,128)} %trailing_hbm.3), custom_call_target="tpu_custom_call" | custom-call | tf_op jit(solution)/shard_map/products/pallas_call | solution.py:121
  9.1 0.0 copy-start
  9.1 25.8 %all_to_all.10.in_ref = f32[32,24,128]{2,1,0:T(8,128)S(1)} all-to-all(f32[32,24,128]{2,1,0:T(8,128)} %products.1), channel_id=1, replica_groups=mesh['rows'=32,'cols'=8] {'rows'}, dimensions={0} | all-to-all | bytes 786432 | tf_op jit(solution)/shard_map/all_to_all | solution.py:389
  34.9 0.1 sum_parts.1
  35.0 17.7 %all_to_all.11.own_ref = f32[32,24,128]{2,1,0:T(8,128)S(1)} all-to-all(f32[32,24,128]{2,1,0:T(8,128)S(1)} %sum_parts.1), channel_id=1, replica_groups=mesh['rows'=32,'cols'=8] {'rows'}, dimensions={0} | all-to-all | bytes 786432 | tf_op jit(solution)/shard_map/all_to_all | solution.py:391
  52.7 3.3 %collective-permute-start = (f32[32,24,128]{2,1,0:T(8,128)S(1)}, f32[32,24,128]{2,1,0:T(8,128)S(1)}, u32[]{:S(2)}, u32[]{:S(2)}) collective-permute-start(f32[32,24,128]{2,1,0:T(8,128)S(1)} %all_to_all.11.own_ref), channel_id=1, source_target_pairs={{0,1},{1,0},{2,3},{3,2},{4,5},{5,4},{6,7},{7,6},{8,9},{9,8},{10,11... | collective-permute-start | bytes 1179656 | tf_op jit(solution)/shard_map/ppermute | solution.py:392
  56.0 1.3 %collective-permute-done.other_ref = f32[32,24,128]{2,1,0:T(8,128)S(1)} collective-permute-done((f32[32,24,128]{2,1,0:T(8,128)S(1)}, f32[32,24,128]{2,1,0:T(8,128)S(1)}, u32[]{:S(2)}, u32[]{:S(2)}) %collective-permute-start) | collective-permute-done | bytes 393248 | tf_op jit(solution)/shard_map/ppermute | solution.py:392
  57.4 0.0 copy-done
  57.4 11.4 %factor.1 = (f32[256,256]{1,0:T(8,128)}, f32[256,128]{1,0:T(8,128)}, f32[4096,128]{1,0:T(8,128)}) custom-call(s32[1]{0:T(128)S(6)} %select_n.7.core_ref, f32[32,24,128]{2,1,0:T(8,128)S(1)} %all_to_all.11.own_ref, f32[32,24,128]{2,1,0:T(8,128)S(1)} %collective-permute-done.other_ref, f32[4096,256]{1,0:T(8,128)} %panel_hbm.3, f32[4096,128]{1,0:T(8,128)S(1)} %copy-done), custom_call_target="tpu_custom_call" | custom-call | tf_op jit(solution)/shard_map/factor/pallas_call | solution.py:355
Async XLA Ops:
  9.1 48.3 %copy-start = (f32[4096,128]{1,0:T(8,128)S(1)}, f32[4096,128]{1,0:T(8,128)}, u32[]{:S(2)}) copy-start(f32[4096,128]{1,0:T(8,128)} %trailing_hbm.3) | copy-start | bytes 6291460
  52.7 4.7 %collective-permute-start = (f32[32,24,128]{2,1,0:T(8,128)S(1)}, f32[32,24,128]{2,1,0:T(8,128)S(1)}, u32[]{:S(2)}, u32[]{:S(2)}) collective-permute-start(f32[32,24,128]{2,1,0:T(8,128)S(1)} %all_to_all.11.own_ref), channel_id=1, source_target_pairs={{0,1},{1,0},{2,3},{3,2},{4,5},{5,4},{6,7},{7,6},{8,9},{9,8},{10,11... | collective-permute-start | bytes 1179656 | tf_op jit(solution)/shard_map/ppermute | solution.py:392

commit v3 on v2

--- a/solution.py
+++ b/solution.py
@@ -88,10 +88,19 @@
         a = grid_split(panel[rows, :], 6)
         t = split3(trailing[rows, :])
         b = [
-            jnp.concatenate([jnp.where(first_core, x[:, 0:H], x[:, H:N]), y], axis=1)
+            (
+                jnp.concatenate([x[:, 0:H], y], axis=1),
+                jnp.concatenate([jnp.where(first_core, x[:, 0:H], x[:, H:N]), y], axis=1),
+            )
             for x, y in zip(a, t)
         ]
         return a, b
+
+    def halves(a, *b):
+        return jnp.concatenate(
+            [dot_t(a[:, 0:H], jnp.concatenate([x[0] for x in b], axis=1)), dot_t(a[:, H:N], jnp.concatenate([x[1] for x in b], axis=1))],
+            axis=0,
+        )
 
     for copy in first:
         copy.wait()
@@ -103,14 +112,17 @@
         (a1, a2, a3), (b1, b2, b3) = held
         if i + 1 < chunks:
             held = split(i + 1)
-        one = dot_t(a1, jnp.concatenate([b1, b2, b3], axis=1))
-        two = dot_t(a2, jnp.concatenate([b1, b2, a3], axis=1))
-        rest = rest + (one[:, N : 2 * N] + one[:, 2 * N :] + (two[:, 0:N] + two[:, N : 2 * N] + dot_t(a3, b1)))
+        one = halves(a1, b1, b2, b3)
+        two = halves(a2, b1, b2, (a3, a3))
+        rest = rest + (one[:, N : 2 * N] + one[:, 2 * N :] + (two[:, 0:N] + two[:, N : 2 * N] + halves(a3, b1)))
         mixed = mixed + two[:, 2 * N :]
         hi, e = two_sum(hi, one[:, 0:N])
         lo = lo + e
     mixed = mixed + mixed.T
-    s, e = two_sum(hi[:, 0:H], rest[:, 0:H] + jnp.where(first_core, mixed[:, 0:H], mixed[:, H:N]))
+    mixed = jnp.concatenate(
+        [mixed[0:H, 0:H], jnp.where(first_core, mixed[H:N, 0:H], mixed[H:N, H:N])], axis=0
+    )
+    s, e = two_sum(hi[:, 0:H], rest[:, 0:H] + mixed)
     out_ref[:, 0:8, :] = s.reshape(RING, 8, H)
     out_ref[:, 8:16, :] = (lo[:, 0:H] + e).reshape(RING, 8, H)
     out_ref[:, 16:24, :] = (hi[:, H:N] + (lo[:, H:N] + rest[:, H:N])).reshape(RING, 8, H)
@@ -132,7 +144,7 @@
             pltpu.VMEM((rows, H), F32),
             pltpu.SemaphoreType.DMA((2, 2)),
         ],
-        compiler_params=pltpu.CompilerParams(vmem_limit_bytes=60 * 1024 * 1024),
+        compiler_params=pltpu.CompilerParams(vmem_limit_bytes=105 * 512 * 1024),
         name="products",
     )(core, panel, trailing)
 
@@ -163,18 +175,12 @@
 
 
 def eliminate(g, b):
+    group, slack, depth = 2, 2, 1
     sub = lax.broadcasted_iota(jnp.int32, (8, H), 0)
-    group, slack, depth = 2, 2, 1
-    blocks = N // 8
-    half = blocks // 2
-
-    def groups_of(t):
-        return [(g, 0), (g, 1), (b, 0)] if t < half else [(g, 1), (b, 0), (b, 1)]
-
-    def spread(rows, groups, column):
-        q = [i for i, (ref, p) in enumerate(groups) if ref is g and p == column // H][0]
-        lane = column % H
-        return jnp.broadcast_to(rows[q][:, lane : lane + 1], (8, H))
+    blocks = H // 8
+
+    def spread(rows, column):
+        return jnp.broadcast_to(rows[0][:, column : column + 1], (8, H))
 
     def over(x, j):
         return jnp.broadcast_to(x[j : j + 1, :], (8, H))
@@ -182,15 +188,12 @@
     x, done = [], []
     for t in range(blocks):
         window = group - t % group + slack
-        groups = groups_of(t)
         wide = [w for w in range(window) if t + w < blocks]
-        rows = [
-            [ref[8 * (t + w) : 8 * (t + w) + 8, H * p : H * p + H] for ref, p in groups] for w in wide
-        ]
+        rows = [[ref[8 * (t + w) : 8 * (t + w) + 8, :] for ref in (g, b)] for w in wide]
         for w in wide[len(x) :]:
-            x.append([spread(rows[w], groups, 8 * t + k) for k in range(8)])
+            x.append([spread(rows[w], 8 * t + k) for k in range(8)])
         near = wide[1 : 1 + depth]
-        ahead = [None] + [[spread(rows[w], groups, 8 * t + 8 + k) for k in range(8)] for w in near]
+        ahead = [None] + [[spread(rows[w], 8 * t + 8 + k) for k in range(8)] for w in near]
         d = over(x[0][0], 0)
         scale = jnp.zeros((8, H), F32)
         for k in range(8):
@@ -210,36 +213,57 @@
                     for w in near:
                         ahead[w][j] = ahead[w][j] - x[w][k] * f
             u[0] = jnp.where(sub > k, u[0], F32(0.0))
-            for q in range(3):
+            for q in range(2):
                 line = over(rows[0][q], k)
                 for w in wide:
                     rows[w][q] = rows[w][q] - u[w] * line
         rows[0] = [piece * scale for piece in rows[0]]
         for w in wide:
-            for q, (ref, p) in enumerate(groups):
-                ref[8 * (t + w) : 8 * (t + w) + 8, H * p : H * p + H] = rows[w][q]
+            for q, ref in enumerate((g, b)):
+                ref[8 * (t + w) : 8 * (t + w) + 8, :] = rows[w][q]
         x = ahead[1:]
         done.append(jnp.concatenate(rows[0], axis=1))
-        first = 8 * (t + 1 + slack)
         if t % group < group - 1:
             continue
-        if first < N:
+        first = 8 * (t + 1 + slack)
+        if first < H:
             u1, u2, u3 = split3(jnp.concatenate(done, axis=0))
             left = jnp.concatenate([u1, u1, u2, u1, u2, u3], axis=0)
             right = jnp.concatenate([u1, u2, u1, u3, u2, u1], axis=0)
-            for part in range(2):
-                top, end = max(first, H * part), H * part + H
-                if top >= end:
-                    continue
-                q = [i for i, (ref, p) in enumerate(groups) if ref is g and p == part][0]
-                change = dot_t(left[:, H * q : H * q + H], right)
-                for i, (ref, p) in enumerate(groups):
-                    stop = min(end, H + 8 * (group + slack)) if ref is g and p < part else end
-                    if top < stop:
-                        ref[top:stop, H * p : H * p + H] -= change[
-                            top - H * part : stop - H * part, H * i : H * i + H
-                        ]
+            change = dot_t(left[:, 0:H], right)
+            g[first:H, :] -= change[first:H, 0:H]
+            b[first:H, :] -= change[first:H, H:N]
         done = []
+
+
+def triangles(g, b):
+    row = lax.broadcasted_iota(jnp.int32, (H, H), 0)
+    col = lax.broadcasted_iota(jnp.int32, (H, H), 1)
+    return jnp.where(row <= col, g[...], F32(0.0)), jnp.where(row >= col, b[...], F32(0.0))
+
+
+def identity():
+    row = lax.broadcasted_iota(jnp.int32, (H, H), 0)
+    col = lax.broadcasted_iota(jnp.int32, (H, H), 1)
+    return jnp.where(row == col, F32(1.0), F32(0.0))
+
+
+def first_kernel(own_ref, out_ref, g, b):
+    g[...] = own_ref[0 : RING // 2, 0:8, :].reshape(H, H)
+    b[...] = identity()
+    eliminate(g, b)
+    out_ref[0], out_ref[1] = triangles(g, b)
+
+
+def first_half(own):
+    return pl.pallas_call(
+        first_kernel,
+        out_shape=jax.ShapeDtypeStruct((2, H, H), F32),
+        scratch_shapes=[pltpu.VMEM((H, H), F32)] * 2,
+        compiler_params=pltpu.CompilerParams(vmem_limit_bytes=VMEM),
+        cost_estimate=pl.CostEstimate(flops=40_000_000, bytes_accessed=10_000_000, transcendentals=0),
+        name="first_half",
+    )(own)
 
 
 def product3(dot, a, b):
@@ -255,8 +279,8 @@
 
 
 def factor_kernel(
-    core_ref, own_ref, other_ref, panel_hbm, trailing_hbm, factor_hbm, proj_hbm, rest_hbm,
-    panel, trailing, rest, factor_ref, proj_ref, hi, lo, g, b, xs, qs, in_sems, out_sems,
+    core_ref, own_ref, other_ref, first_ref, panel_hbm, trailing_hbm, factor_hbm, proj_hbm, rest_hbm,
+    panel, trailing, rest, factor_ref, proj_ref, g, b, xs, qs, in_sems, out_sems,
 ):
     loads = (
         pltpu.make_async_copy(panel_hbm, panel, in_sems.at[0]),
@@ -265,28 +289,48 @@
     for copy in loads:
         copy.start()
     first_core = core_ref[0] == 0
-    for ref, at in ((hi, 0), (lo, 8)):
+    quarters = []
+    for at in (0, 8):
         mine = own_ref[:, at : at + 8, :].reshape(N, H)
-        theirs = other_ref[:, at : at + 8, :].reshape(N, H)
-        ref[:, 0:H] = jnp.where(first_core, mine, theirs)
-        ref[:, H:N] = jnp.where(first_core, theirs, mine)
+        theirs = other_ref[:, at : at + 8, :].reshape(N, H)[H:N]
+        top, mine = mine[0:H], mine[H:N]
+        quarters.append((top, jnp.where(first_core, mine, theirs), jnp.where(first_core, theirs, mine)))
+    (hi00, hi10, hi11), (lo00, lo10, lo11) = quarters
     c = own_ref[:, 16:24, :].reshape(N, H)
-    g[...] = hi[...]
     row = lax.broadcasted_iota(jnp.int32, (N, N), 0)
     col = lax.broadcasted_iota(jnp.int32, (N, N), 1)
-    b[...] = jnp.where(row == col, F32(1.0), F32(0.0))
+    u00, w00 = first_ref[0], first_ref[1]
+    w00s = split3(w00)
+    u01 = product6s(dot_r, w00s, split3(hi10))
+    u01s = split3(u01)
+    g[...] = hi11 - product6s(dot_t, u01s, u01s)
+    b[...] = identity()
     eliminate(g, b)
-
-    upper = jnp.where(row <= col, g[...], F32(0.0))
-    inverse = jnp.where(row >= col, b[...], F32(0.0))
+    u11, w11 = triangles(g, b)
+    w10 = -product6(dot_n, w11, product6s(dot_t, u01s, w00s))
+    zero = jnp.zeros((H, H), F32)
+
+    def whole(a00, a01, a10, a11):
+        return jnp.concatenate(
+            [jnp.concatenate([a00, a01], axis=1), jnp.concatenate([a10, a11], axis=1)], axis=0
+        )
+
+    upper = whole(u00, u01, zero, u11)
+    inverse = whole(w00, zero, w10, w11)
     w1, w2, w3 = split3(inverse)
     y = product6s(dot_n, (w1, w2, w3), split3(c))
     u1, u2, u3 = grid_split(upper, 7)
     exact = dot_t(u1, u1)
     v = (dot_t(u1, u2) + dot_t(u1, u3)) + (dot_t(u2, u2 * BF16(0.5)) + dot_t(u2, u3))
-    d = ((hi[...] - exact) + lo[...]) - (v + v.T)
+    v = v + v.T
+    d00 = ((hi00 - exact[0:H, 0:H]) + lo00) - v[0:H, 0:H]
+    d10 = ((hi10 - exact[H:N, 0:H]) + lo10) - v[H:N, 0:H]
+    d11 = ((hi11 - exact[H:N, H:N]) + lo11) - v[H:N, H:N]
+    d = whole(d00, d10.T, d10, d11)
     f = product3(dot_n, (w1, w2), split2(d))
     e = product3(dot_r, split2(f), (w1, w2))
+    miss = product6s(dot_r, (w1, w2, w3), split3(upper)) - jnp.where(row == col, F32(1.0), F32(0.0))
+    e = e + (miss + miss.T)
     size = jnp.max(jnp.sum(jnp.abs(e), axis=0, keepdims=True))
     lower = jnp.where(row > col, F32(1.0), jnp.where(row == col, F32(0.5), F32(0.0)))
     es = split2(e)
@@ -317,9 +361,9 @@
         qs[...] = q
 
     q = qs[...]
-    xb = split2(xs[...])
+    xb = split2(xs[...] - miss)
     z1, z2, z3 = split3(product6s(dot_t, (w1, w2, w3), split3(q)))
-    proj_ref[...] = q + product3(dot_t, xb, split2(q))
+    proj_ref[...] = q + product3(dot_t, split2(xs[...]), split2(q))
     factor_ref[...] = upper + product3(dot_t, xb, split2(upper))
     strips = panel.shape[0] // STRIP
     stores = [
@@ -350,12 +394,12 @@
         copy.wait()
 
 
-def factor(core, own, other, panel, trailing):
+def factor(core, own, other, first, panel, trailing):
     rows = panel.shape[0]
     return pl.pallas_call(
         factor_kernel,
         in_specs=[pl.BlockSpec(memory_space=pltpu.SMEM)]
-        + [pl.BlockSpec(memory_space=pltpu.VMEM)] * 2
+        + [pl.BlockSpec(memory_space=pltpu.VMEM)] * 3
         + [pl.BlockSpec(memory_space=pl.ANY)] * 2,
         out_specs=[pl.BlockSpec(memory_space=pl.ANY)] * 3,
         out_shape=(
@@ -369,10 +413,8 @@
             pltpu.VMEM((rows, H), F32),
             pltpu.VMEM((N, N), F32),
             pltpu.VMEM((N, H), F32),
-            pltpu.VMEM((N, N), F32),
-            pltpu.VMEM((N, N), F32),
-            pltpu.VMEM((N, N), F32),
-            pltpu.VMEM((N, N), F32),
+            pltpu.VMEM((H, H), F32),
+            pltpu.VMEM((H, H), F32),
             pltpu.VMEM((N, N), F32),
             pltpu.VMEM((N, H), F32),
             pltpu.SemaphoreType.DMA((2,)),
@@ -380,7 +422,7 @@
         ],
         compiler_params=pltpu.CompilerParams(vmem_limit_bytes=VMEM),
         name="factor",
-    )(core, own, other, panel, trailing)
+    )(core, own, other, first, panel, trailing)
 
 
 def on_device(panel, trailing):
@@ -390,7 +432,8 @@
     summed = sum_parts(received)
     own = lax.all_to_all(summed, "rows", 0, 0, tiled=True)
     other = lax.ppermute(own, "cols", [(j, j ^ 1) for j in range(lax.axis_size("cols"))])
-    return tuple(factor(core, own, other, panel, trailing))
+    first = first_half(own)
+    return tuple(factor(core, own, other, first, panel, trailing))
 
 
 def solution(mesh):

time: 69.2 us -> 71.3 us (1.030)
  Pallas kernels: 19.9 us -> 23.6 us
  waiting for transfers between devices: 1.35 us -> 0.01 us
    pallas_call x0 -> x1, Pallas kernels: none -> 2.28 us  [first_half(): pl.pallas_call(first_kernel, out_shape=jax.ShapeDtypeStruct((2, H, H), F3...]
    pallas_call x1, Pallas kernels: 11.4 us -> 13.3 us  [factor(): pl.pallas_call(factor_kernel, in_specs=[pl.BlockSpec(memory_space=pltpu.S...]
    ppermute x1, waiting for transfers between devices: 1.35 us -> 0.01 us  [on_device(): lax.ppermute(own, 'cols', [(j, j ^ 1) for j in range(lax.axis_size('cols'...]
  transfers between devices with their start and end apart: 1 -> 1, of which waited for: 1 -> 0; matrix products, arithmetic and copies ran while one was open for 0% -> 0% of each run, Pallas kernels for 0% -> 3%
where the time goes in v3:
time: 71.3 us; the launch traced here: 71.1 us
  blocking collectives  43.3 us (61%)
  Pallas kernels  23.6 us (33%)
  starting transfers between devices  3.34 us (5%)
  between operations  0.84 us (1%)
    all_to_all x1, blocking collectives, on_device(): received = lax.all_to_all(sent, 'rows', 0, 0, tiled=True)  25.6 us
    all_to_all x1, blocking collectives, on_device(): own = lax.all_to_all(summed, 'rows', 0, 0, tiled=True)  17.7 us
    pallas_call x1, Pallas kernels, factor(): pl.pallas_call(factor_kernel, in_specs=[pl.BlockSpec(memory_space=pltpu.S...  13.3 us
    pallas_call x1, Pallas kernels, gram(): pl.pallas_call(gram_kernel, in_specs=[pl.BlockSpec(memory_space=pltpu.SME...  7.92 us
    ppermute x1, starting transfers between devices, on_device(): lax.ppermute(own, 'cols', [(j, j ^ 1) for j in range(lax.axis_size('cols'...  3.34 us
    pallas_call x1, Pallas kernels, first_half(): pl.pallas_call(first_kernel, out_shape=jax.ShapeDtypeStruct((2, H, H), F3...  2.28 us
  transfers between devices with their start and end apart: 1, of which 0 were waited for; matrix products, arithmetic and copies ran while one was open for 0% of the time, Pallas kernels for 3%

profile of v3, /device:TPU:1, one launch (start us, length us, event | category | flops | bytes accessed | tf_op | source)
XLA Modules:
  0.0 71.1 jit_solution(6690804488349614898)
XLA Ops:
  0.6 7.9 %products.1 = f32[32,24,128]{2,1,0:T(8,128)S(1)} custom-call(s32[1]{0:T(128)S(6)} %select_n.7.core_ref, f32[4096,256]{1,0:T(8,128)} %panel_hbm.3, f32[4096,128]{1,0:T(8,128)} %trailing_hbm.3), custom_call_target="tpu_custom_call" | custom-call | tf_op jit(solution)/shard_map/products/pallas_call | solution.py:133
  8.6 0.0 copy-start
  8.6 25.6 %all_to_all.10.in_ref = f32[32,24,128]{2,1,0:T(8,128)S(1)} all-to-all(f32[32,24,128]{2,1,0:T(8,128)S(1)} %products.1), channel_id=1, replica_groups=mesh['rows'=32,'cols'=8] {'rows'}, dimensions={0} | all-to-all | bytes 786432 | tf_op jit(solution)/shard_map/all_to_all | solution.py:431
  34.2 0.1 sum_parts.1
  34.3 17.7 %all_to_all.11.own_ref = f32[32,24,128]{2,1,0:T(8,128)S(1)} all-to-all(f32[32,24,128]{2,1,0:T(8,128)S(1)} %sum_parts.1), channel_id=1, replica_groups=mesh['rows'=32,'cols'=8] {'rows'}, dimensions={0} | all-to-all | bytes 786432 | tf_op jit(solution)/shard_map/all_to_all | solution.py:433
  51.9 3.3 %collective-permute-start = (f32[32,24,128]{2,1,0:T(8,128)S(1)}, f32[32,24,128]{2,1,0:T(8,128)S(1)}, u32[]{:S(2)}, u32[]{:S(2)}) collective-permute-start(f32[32,24,128]{2,1,0:T(8,128)S(1)} %all_to_all.11.own_ref), channel_id=1, source_target_pairs={{0,1},{1,0},{2,3},{3,2},{4,5},{5,4},{6,7},{7,6},{8,9},{9,8},{10,11... | collective-permute-start | bytes 1179656 | tf_op jit(solution)/shard_map/ppermute | solution.py:434
  55.3 2.3 %first_half.1.first_ref = f32[2,128,128]{2,1,0:T(8,128)S(1)} custom-call(f32[32,24,128]{2,1,0:T(8,128)S(1)} %all_to_all.11.own_ref), custom_call_target="tpu_custom_call" | custom-call | flops 40000000 | bytes 10000000 | tf_op jit(solution)/shard_map/first_half/pallas_call | solution.py:259
  57.6 0.0 collective-permute-done.other_ref
  57.6 0.0 copy-done
  57.6 13.3 %factor.1 = (f32[256,256]{1,0:T(8,128)}, f32[256,128]{1,0:T(8,128)}, f32[4096,128]{1,0:T(8,128)}) custom-call(s32[1]{0:T(128)S(6)} %select_n.7.core_ref, f32[32,24,128]{2,1,0:T(8,128)S(1)} %all_to_all.11.own_ref, f32[32,24,128]{2,1,0:T(8,128)S(1)} %collective-permute-done.other_ref, f32[2,128,128]{2,1,0:T(8,128)S(1)} %first_half.1.first_ref, ...), custom_call_target="tpu_custom_call" | custom-call | tf_op jit(solution)/shard_map/factor/pallas_call | solution.py:399
Async XLA Ops:
  8.6 49.0 %copy-start = (f32[4096,128]{1,0:T(8,128)S(1)}, f32[4096,128]{1,0:T(8,128)}, u32[]{:S(2)}) copy-start(f32[4096,128]{1,0:T(8,128)} %trailing_hbm.3) | copy-start | bytes 6291460
  51.9 5.6 %collective-permute-start = (f32[32,24,128]{2,1,0:T(8,128)S(1)}, f32[32,24,128]{2,1,0:T(8,128)S(1)}, u32[]{:S(2)}, u32[]{:S(2)}) collective-permute-start(f32[32,24,128]{2,1,0:T(8,128)S(1)} %all_to_all.11.own_ref), channel_id=1, source_target_pairs={{0,1},{1,0},{2,3},{3,2},{4,5},{5,4},{6,7},{7,6},{8,9},{9,8},{10,11... | collective-permute-start | bytes 1179656 | tf_op jit(solution)/shard_map/ppermute | solution.py:434

commit v4 on v3

--- a/solution.py
+++ b/solution.py
@@ -331,7 +331,7 @@
     e = product3(dot_r, split2(f), (w1, w2))
     miss = product6s(dot_r, (w1, w2, w3), split3(upper)) - jnp.where(row == col, F32(1.0), F32(0.0))
     e = e + (miss + miss.T)
-    size = jnp.max(jnp.sum(jnp.abs(e), axis=0, keepdims=True))
+    size = jnp.sum(jnp.sum(e * e, axis=0, keepdims=True))
     lower = jnp.where(row > col, F32(1.0), jnp.where(row == col, F32(0.5), F32(0.0)))
     es = split2(e)
     ee = product3(dot_n, es, es)
@@ -343,7 +343,7 @@
     xs[...] = x
     qs[...] = q
 
-    @pl.when(jnp.logical_not(size < F32(0.03)))
+    @pl.when(jnp.logical_not(size < F32(0.05**2)))
     def _():
         def again(state):
             old, _, count = state

time: 71.3 us -> 67.3 us (0.944)
  Pallas kernels: 23.6 us -> 19.7 us
    pallas_call x1, Pallas kernels: 13.3 us -> 9.42 us  [factor(): pl.pallas_call(factor_kernel, in_specs=[pl.BlockSpec(memory_space=pltpu.S...]
where the time goes in v4:
time: 67.3 us; the launch traced here: 67.2 us
  blocking collectives  43.3 us (64%)
  Pallas kernels  19.7 us (29%)
  starting transfers between devices  3.34 us (5%)
  between operations  0.84 us (1%)
    all_to_all x1, blocking collectives, on_device(): received = lax.all_to_all(sent, 'rows', 0, 0, tiled=True)  25.6 us
    all_to_all x1, blocking collectives, on_device(): own = lax.all_to_all(summed, 'rows', 0, 0, tiled=True)  17.7 us
    pallas_call x1, Pallas kernels, factor(): pl.pallas_call(factor_kernel, in_specs=[pl.BlockSpec(memory_space=pltpu.S...  9.42 us
    pallas_call x1, Pallas kernels, gram(): pl.pallas_call(gram_kernel, in_specs=[pl.BlockSpec(memory_space=pltpu.SME...  7.92 us
    ppermute x1, starting transfers between devices, on_device(): lax.ppermute(own, 'cols', [(j, j ^ 1) for j in range(lax.axis_size('cols'...  3.34 us
    pallas_call x1, Pallas kernels, first_half(): pl.pallas_call(first_kernel, out_shape=jax.ShapeDtypeStruct((2, H, H), F3...  2.28 us
  transfers between devices with their start and end apart: 1, of which 0 were waited for; matrix products, arithmetic and copies ran while one was open for 0% of the time, Pallas kernels for 3%

profile of v4, /device:TPU:1, one launch (start us, length us, event | category | flops | bytes accessed | tf_op | source)
XLA Modules:
  0.0 67.2 jit_solution(1808756397846894613)
XLA Ops:
  0.6 7.9 %products.1 = f32[32,24,128]{2,1,0:T(8,128)S(1)} custom-call(s32[1]{0:T(128)S(6)} %select_n.7.core_ref, f32[4096,256]{1,0:T(8,128)} %panel_hbm.3, f32[4096,128]{1,0:T(8,128)} %trailing_hbm.3), custom_call_target="tpu_custom_call" | custom-call | tf_op jit(solution)/shard_map/products/pallas_call | solution.py:133
  8.6 0.0 copy-start
  8.6 25.6 %all_to_all.10.in_ref = f32[32,24,128]{2,1,0:T(8,128)S(1)} all-to-all(f32[32,24,128]{2,1,0:T(8,128)S(1)} %products.1), channel_id=1, replica_groups=mesh['rows'=32,'cols'=8] {'rows'}, dimensions={0} | all-to-all | bytes 786432 | tf_op jit(solution)/shard_map/all_to_all | solution.py:431
  34.2 0.1 sum_parts.1
  34.3 17.7 %all_to_all.11.own_ref = f32[32,24,128]{2,1,0:T(8,128)S(1)} all-to-all(f32[32,24,128]{2,1,0:T(8,128)S(1)} %sum_parts.1), channel_id=1, replica_groups=mesh['rows'=32,'cols'=8] {'rows'}, dimensions={0} | all-to-all | bytes 786432 | tf_op jit(solution)/shard_map/all_to_all | solution.py:433
  51.9 3.3 %collective-permute-start = (f32[32,24,128]{2,1,0:T(8,128)S(1)}, f32[32,24,128]{2,1,0:T(8,128)S(1)}, u32[]{:S(2)}, u32[]{:S(2)}) collective-permute-start(f32[32,24,128]{2,1,0:T(8,128)S(1)} %all_to_all.11.own_ref), channel_id=1, source_target_pairs={{0,1},{1,0},{2,3},{3,2},{4,5},{5,4},{6,7},{7,6},{8,9},{9,8},{10,11... | collective-permute-start | bytes 1179656 | tf_op jit(solution)/shard_map/ppermute | solution.py:434
  55.3 2.3 %first_half.1.first_ref = f32[2,128,128]{2,1,0:T(8,128)S(1)} custom-call(f32[32,24,128]{2,1,0:T(8,128)S(1)} %all_to_all.11.own_ref), custom_call_target="tpu_custom_call" | custom-call | flops 40000000 | bytes 10000000 | tf_op jit(solution)/shard_map/first_half/pallas_call | solution.py:259
  57.6 0.0 collective-permute-done.other_ref
  57.6 0.0 copy-done
  57.6 9.4 %factor.1 = (f32[256,256]{1,0:T(8,128)}, f32[256,128]{1,0:T(8,128)}, f32[4096,128]{1,0:T(8,128)}) custom-call(s32[1]{0:T(128)S(6)} %select_n.7.core_ref, f32[32,24,128]{2,1,0:T(8,128)S(1)} %all_to_all.11.own_ref, f32[32,24,128]{2,1,0:T(8,128)S(1)} %collective-permute-done.other_ref, f32[2,128,128]{2,1,0:T(8,128)S(1)} %first_half.1.first_ref, ...), custom_call_target="tpu_custom_call" | custom-call | tf_op jit(solution)/shard_map/factor/pallas_call | solution.py:399
Async XLA Ops:
  8.6 49.0 %copy-start = (f32[4096,128]{1,0:T(8,128)S(1)}, f32[4096,128]{1,0:T(8,128)}, u32[]{:S(2)}) copy-start(f32[4096,128]{1,0:T(8,128)} %trailing_hbm.3) | copy-start | bytes 6291460
  51.9 5.6 %collective-permute-start = (f32[32,24,128]{2,1,0:T(8,128)S(1)}, f32[32,24,128]{2,1,0:T(8,128)S(1)}, u32[]{:S(2)}, u32[]{:S(2)}) collective-permute-start(f32[32,24,128]{2,1,0:T(8,128)S(1)} %all_to_all.11.own_ref), channel_id=1, source_target_pairs={{0,1},{1,0},{2,3},{3,2},{4,5},{5,4},{6,7},{7,6},{8,9},{9,8},{10,11... | collective-permute-start | bytes 1179656 | tf_op jit(solution)/shard_map/ppermute | solution.py:434

commit v5 on v4

--- a/solution.py
+++ b/solution.py
@@ -248,8 +248,8 @@
     return jnp.where(row == col, F32(1.0), F32(0.0))
 
 
-def first_kernel(own_ref, out_ref, g, b):
-    g[...] = own_ref[0 : RING // 2, 0:8, :].reshape(H, H)
+def first_kernel(top_ref, out_ref, g, b):
+    g[...] = top_ref[...].reshape(H, H)
     b[...] = identity()
     eliminate(g, b)
     out_ref[0], out_ref[1] = triangles(g, b)
@@ -258,6 +258,9 @@
 def first_half(own):
     return pl.pallas_call(
         first_kernel,
+        grid=(1,),
+        in_specs=[pl.BlockSpec((RING // 2, 8, H), lambda i: (0, 0, 0))],
+        out_specs=pl.BlockSpec((2, H, H), lambda i: (0, 0, 0)),
         out_shape=jax.ShapeDtypeStruct((2, H, H), F32),
         scratch_shapes=[pltpu.VMEM((H, H), F32)] * 2,
         compiler_params=pltpu.CompilerParams(vmem_limit_bytes=VMEM),
@@ -292,7 +295,7 @@
     quarters = []
     for at in (0, 8):
         mine = own_ref[:, at : at + 8, :].reshape(N, H)
-        theirs = other_ref[:, at : at + 8, :].reshape(N, H)[H:N]
+        theirs = other_ref[:, at : at + 8, :].reshape(H, H)
         top, mine = mine[0:H], mine[H:N]
         quarters.append((top, jnp.where(first_core, mine, theirs), jnp.where(first_core, theirs, mine)))
     (hi00, hi10, hi11), (lo00, lo10, lo11) = quarters
@@ -398,8 +401,13 @@
     rows = panel.shape[0]
     return pl.pallas_call(
         factor_kernel,
+        grid=(1,),
         in_specs=[pl.BlockSpec(memory_space=pltpu.SMEM)]
-        + [pl.BlockSpec(memory_space=pltpu.VMEM)] * 3
+        + [
+            pl.BlockSpec(memory_space=pltpu.VMEM),
+            pl.BlockSpec((RING // 2, 16, H), lambda i: (1, 0, 0)),
+            pl.BlockSpec(memory_space=pltpu.VMEM),
+        ]
         + [pl.BlockSpec(memory_space=pl.ANY)] * 2,
         out_specs=[pl.BlockSpec(memory_space=pl.ANY)] * 3,
         out_shape=(

time: 67.3 us -> 67.3 us (level)
  no operation moved by 1% of the time
where the time goes in v5:
time: 67.3 us; the launch traced here: 67.2 us
  blocking collectives  43.3 us (64%)
  Pallas kernels  19.7 us (29%)
  starting transfers between devices  3.34 us (5%)
  between operations  0.84 us (1%)
    all_to_all x1, blocking collectives, on_device(): received = lax.all_to_all(sent, 'rows', 0, 0, tiled=True)  25.6 us
    all_to_all x1, blocking collectives, on_device(): own = lax.all_to_all(summed, 'rows', 0, 0, tiled=True)  17.7 us
    pallas_call x1, Pallas kernels, factor(): pl.pallas_call(factor_kernel, grid=(1,), in_specs=[pl.BlockSpec(memory_sp...  9.43 us
    pallas_call x1, Pallas kernels, gram(): pl.pallas_call(gram_kernel, in_specs=[pl.BlockSpec(memory_space=pltpu.SME...  7.92 us
    ppermute x1, starting transfers between devices, on_device(): lax.ppermute(own, 'cols', [(j, j ^ 1) for j in range(lax.axis_size('cols'...  3.34 us
    pallas_call x1, Pallas kernels, first_half(): pl.pallas_call(first_kernel, grid=(1,), in_specs=[pl.BlockSpec((RING // 2...  2.28 us
  transfers between devices with their start and end apart: 1, of which 0 were waited for; matrix products, arithmetic and copies ran while one was open for 0% of the time, Pallas kernels for 3%

profile of v5, /device:TPU:1, one launch (start us, length us, event | category | flops | bytes accessed | tf_op | source)
XLA Modules:
  0.0 67.2 jit_solution(5463644791451939103)
XLA Ops:
  0.6 7.9 %products.1 = f32[32,24,128]{2,1,0:T(8,128)S(1)} custom-call(s32[1]{0:T(128)S(6)} %select_n.7.core_ref, f32[4096,256]{1,0:T(8,128)} %panel_hbm.3, f32[4096,128]{1,0:T(8,128)} %trailing_hbm.3), custom_call_target="tpu_custom_call" | custom-call | tf_op jit(solution)/shard_map/products/pallas_call | solution.py:133
  8.6 0.0 copy-start
  8.6 25.6 %all_to_all.10.in_ref = f32[32,24,128]{2,1,0:T(8,128)S(1)} all-to-all(f32[32,24,128]{2,1,0:T(8,128)S(1)} %products.1), channel_id=1, replica_groups=mesh['rows'=32,'cols'=8] {'rows'}, dimensions={0} | all-to-all | bytes 786432 | tf_op jit(solution)/shard_map/all_to_all | solution.py:439
  34.2 0.1 sum_parts.1
  34.3 17.7 %all_to_all.11.top_ref.own_ref = f32[32,24,128]{2,1,0:T(8,128)S(1)} all-to-all(f32[32,24,128]{2,1,0:T(8,128)S(1)} %sum_parts.1), channel_id=1, replica_groups=mesh['rows'=32,'cols'=8] {'rows'}, dimensions={0} | all-to-all | bytes 786432 | tf_op jit(solution)/shard_map/all_to_all | solution.py:441
  51.9 3.3 %collective-permute-start = (f32[32,24,128]{2,1,0:T(8,128)S(1)}, f32[32,24,128]{2,1,0:T(8,128)S(1)}, u32[]{:S(2)}, u32[]{:S(2)}) collective-permute-start(f32[32,24,128]{2,1,0:T(8,128)S(1)} %all_to_all.11.top_ref.own_ref), channel_id=1, source_target_pairs={{0,1},{1,0},{2,3},{3,2},{4,5},{5,4},{6,7},{7,6},{8,9},{9,8},{10,11... | collective-permute-start | bytes 1179656 | tf_op jit(solution)/shard_map/ppermute | solution.py:442
  55.3 2.3 %first_half.1.first_ref = f32[2,128,128]{2,1,0:T(8,128)S(1)} custom-call(f32[32,24,128]{2,1,0:T(8,128)S(1)} %all_to_all.11.top_ref.own_ref), custom_call_target="tpu_custom_call" | custom-call | flops 40000000 | bytes 10000000 | tf_op jit(solution)/shard_map/first_half/pallas_call | solution.py:259
  57.6 0.0 collective-permute-done.other_ref
  57.6 0.0 copy-done
  57.6 9.4 %factor.1 = (f32[256,256]{1,0:T(8,128)}, f32[256,128]{1,0:T(8,128)}, f32[4096,128]{1,0:T(8,128)}) custom-call(s32[1]{0:T(128)S(6)} %select_n.7.core_ref, f32[32,24,128]{2,1,0:T(8,128)S(1)} %all_to_all.11.top_ref.own_ref, f32[32,24,128]{2,1,0:T(8,128)S(1)} %collective-permute-done.other_ref, f32[2,128,128]{2,1,0:T(8,128)S(1)} %first_half.1.first_ref, ...), custom_call_target="tpu_custom_call" | custom-call | tf_op jit(solution)/shard_map/factor/pallas_call | solution.py:402
Async XLA Ops:
  8.6 49.0 %copy-start = (f32[4096,128]{1,0:T(8,128)S(1)}, f32[4096,128]{1,0:T(8,128)}, u32[]{:S(2)}) copy-start(f32[4096,128]{1,0:T(8,128)} %trailing_hbm.3) | copy-start | bytes 6291460
  51.9 5.6 %collective-permute-start = (f32[32,24,128]{2,1,0:T(8,128)S(1)}, f32[32,24,128]{2,1,0:T(8,128)S(1)}, u32[]{:S(2)}, u32[]{:S(2)}) collective-permute-start(f32[32,24,128]{2,1,0:T(8,128)S(1)} %all_to_all.11.top_ref.own_ref), channel_id=1, source_target_pairs={{0,1},{1,0},{2,3},{3,2},{4,5},{5,4},{6,7},{7,6},{8,9},{9,8},{10,11... | collective-permute-start | bytes 1179656 | tf_op jit(solution)/shard_map/ppermute | solution.py:442

commit v6 on v4

--- a/solution.py
+++ b/solution.py
@@ -363,15 +363,8 @@
     q = qs[...]
     xb = split2(xs[...] - miss)
     z1, z2, z3 = split3(product6s(dot_t, (w1, w2, w3), split3(q)))
-    proj_ref[...] = q + product3(dot_t, split2(xs[...]), split2(q))
-    factor_ref[...] = upper + product3(dot_t, xb, split2(upper))
     strips = panel.shape[0] // STRIP
-    stores = [
-        pltpu.make_async_copy(factor_ref, factor_hbm, out_sems.at[strips]),
-        pltpu.make_async_copy(proj_ref, proj_hbm, out_sems.at[strips + 1]),
-    ]
-    for copy in stores:
-        copy.start()
+    stores = []
     zero = jnp.zeros_like(z1)
     right = jnp.concatenate(
         [
@@ -390,6 +383,13 @@
         store = pltpu.make_async_copy(rest.at[rows], rest_hbm.at[rows], out_sems.at[i])
         store.start()
         stores.append(store)
+        if i == strips // 2:
+            proj_ref[...] = q + product3(dot_t, split2(xs[...]), split2(q))
+            factor_ref[...] = upper + product3(dot_t, xb, split2(upper))
+            for source, target in ((factor_ref, factor_hbm), (proj_ref, proj_hbm)):
+                copy = pltpu.make_async_copy(source, target, out_sems.at[strips + len(stores) - i - 1])
+                copy.start()
+                stores.append(copy)
     for copy in stores:
         copy.wait()
 

time: 67.3 us -> 67.6 us (level)
  no operation moved by 1% of the time
where the time goes in v6:
time: 67.6 us; the launch traced here: 67.4 us
  blocking collectives  43.3 us (64%)
  Pallas kernels  19.9 us (29%)
  starting transfers between devices  3.34 us (5%)
  between operations  0.86 us (1%)
    all_to_all x1, blocking collectives, on_device(): received = lax.all_to_all(sent, 'rows', 0, 0, tiled=True)  25.6 us
    all_to_all x1, blocking collectives, on_device(): own = lax.all_to_all(summed, 'rows', 0, 0, tiled=True)  17.7 us
    pallas_call x1, Pallas kernels, factor(): pl.pallas_call(factor_kernel, in_specs=[pl.BlockSpec(memory_space=pltpu.S...  9.61 us
    pallas_call x1, Pallas kernels, gram(): pl.pallas_call(gram_kernel, in_specs=[pl.BlockSpec(memory_space=pltpu.SME...  7.92 us
    ppermute x1, starting transfers between devices, on_device(): lax.ppermute(own, 'cols', [(j, j ^ 1) for j in range(lax.axis_size('cols'...  3.34 us
    pallas_call x1, Pallas kernels, first_half(): pl.pallas_call(first_kernel, out_shape=jax.ShapeDtypeStruct((2, H, H), F3...  2.28 us
  transfers between devices with their start and end apart: 1, of which 0 were waited for; matrix products, arithmetic and copies ran while one was open for 0% of the time, Pallas kernels for 3%

profile of v6, /device:TPU:1, one launch (start us, length us, event | category | flops | bytes accessed | tf_op | source)
XLA Modules:
  0.0 67.4 jit_solution(2384651027877262132)
XLA Ops:
  0.6 7.9 %products.1 = f32[32,24,128]{2,1,0:T(8,128)S(1)} custom-call(s32[1]{0:T(128)S(6)} %select_n.7.core_ref, f32[4096,256]{1,0:T(8,128)} %panel_hbm.3, f32[4096,128]{1,0:T(8,128)} %trailing_hbm.3), custom_call_target="tpu_custom_call" | custom-call | tf_op jit(solution)/shard_map/products/pallas_call | solution.py:133
  8.6 0.0 copy-start
  8.6 25.6 %all_to_all.10.in_ref = f32[32,24,128]{2,1,0:T(8,128)S(1)} all-to-all(f32[32,24,128]{2,1,0:T(8,128)S(1)} %products.1), channel_id=1, replica_groups=mesh['rows'=32,'cols'=8] {'rows'}, dimensions={0} | all-to-all | bytes 786432 | tf_op jit(solution)/shard_map/all_to_all | solution.py:431
  34.2 0.1 sum_parts.1
  34.3 17.7 %all_to_all.11.own_ref = f32[32,24,128]{2,1,0:T(8,128)S(1)} all-to-all(f32[32,24,128]{2,1,0:T(8,128)S(1)} %sum_parts.1), channel_id=1, replica_groups=mesh['rows'=32,'cols'=8] {'rows'}, dimensions={0} | all-to-all | bytes 786432 | tf_op jit(solution)/shard_map/all_to_all | solution.py:433
  51.9 3.3 %collective-permute-start = (f32[32,24,128]{2,1,0:T(8,128)S(1)}, f32[32,24,128]{2,1,0:T(8,128)S(1)}, u32[]{:S(2)}, u32[]{:S(2)}) collective-permute-start(f32[32,24,128]{2,1,0:T(8,128)S(1)} %all_to_all.11.own_ref), channel_id=1, source_target_pairs={{0,1},{1,0},{2,3},{3,2},{4,5},{5,4},{6,7},{7,6},{8,9},{9,8},{10,11... | collective-permute-start | bytes 1179656 | tf_op jit(solution)/shard_map/ppermute | solution.py:434
  55.3 2.3 %first_half.1.first_ref = f32[2,128,128]{2,1,0:T(8,128)S(1)} custom-call(f32[32,24,128]{2,1,0:T(8,128)S(1)} %all_to_all.11.own_ref), custom_call_target="tpu_custom_call" | custom-call | flops 40000000 | bytes 10000000 | tf_op jit(solution)/shard_map/first_half/pallas_call | solution.py:259
  57.6 0.0 collective-permute-done.other_ref
  57.6 0.0 copy-done
  57.6 9.6 %factor.1 = (f32[256,256]{1,0:T(8,128)}, f32[256,128]{1,0:T(8,128)}, f32[4096,128]{1,0:T(8,128)}) custom-call(s32[1]{0:T(128)S(6)} %select_n.7.core_ref, f32[32,24,128]{2,1,0:T(8,128)S(1)} %all_to_all.11.own_ref, f32[32,24,128]{2,1,0:T(8,128)S(1)} %collective-permute-done.other_ref, f32[2,128,128]{2,1,0:T(8,128)S(1)} %first_half.1.first_ref, ...), custom_call_target="tpu_custom_call" | custom-call | tf_op jit(solution)/shard_map/factor/pallas_call | solution.py:399
Async XLA Ops:
  8.6 49.0 %copy-start = (f32[4096,128]{1,0:T(8,128)S(1)}, f32[4096,128]{1,0:T(8,128)}, u32[]{:S(2)}) copy-start(f32[4096,128]{1,0:T(8,128)} %trailing_hbm.3) | copy-start | bytes 6291460
  51.9 5.6 %collective-permute-start = (f32[32,24,128]{2,1,0:T(8,128)S(1)}, f32[32,24,128]{2,1,0:T(8,128)S(1)}, u32[]{:S(2)}, u32[]{:S(2)}) collective-permute-start(f32[32,24,128]{2,1,0:T(8,128)S(1)} %all_to_all.11.own_ref), channel_id=1, source_target_pairs={{0,1},{1,0},{2,3},{3,2},{4,5},{5,4},{6,7},{7,6},{8,9},{9,8},{10,11... | collective-permute-start | bytes 1179656 | tf_op jit(solution)/shard_map/ppermute | solution.py:434
